TPU v7x, 32 devices: a whole 2x2x4 slice. The times are simulated.
32 devices in a mesh: section: 4 (over x, core), ctx: 2 (over y), dp: 4 (over z).
Axes of the slice: x: 2, y: 2, z: 4, core: 2. Of those that a mesh axis runs over, the one named last changes fastest.
Arguments:
- inputs: bfloat16 [4, 512, 4096], P('section', 'ctx', 'dp'), may hold values from -6 to 6
- upstream: bfloat16 [4, 512, 4096], P('section', 'ctx', 'dp'), may hold values from -6 to 6
- short_filter: bfloat16 [4, 21, 256], P('section', None, 'dp'), may hold values from -2 to 2
- medium_filter: bfloat16 [4, 128, 256], P('section', None, 'dp'), may hold values from -0.5 to 0.5
Outputs:
- incoming: bfloat16 [4, 512, 4096], P('section', 'ctx', 'dp')
- grad_short: float32 [4, 21, 256], P('section', None, ('dp', 'ctx'))
- grad_medium: float32 [4, 128, 256], P('section', None, ('dp', 'ctx'))
All inputs are finite; a program needn't handle non-finite values.
Results may differ from a plain program's by a relative error of at most 0.0071.
Values may be sent and summed in bfloat16 or wider, within the bound.
A program may use at most 64 MiB of HBM per device.

v0:
```python
from functools import partial

import jax
import jax.numpy as jnp
from jax import lax
from jax.sharding import PartitionSpec as P


def passed_along(block, axis, distance):
    devices = range(lax.axis_size(axis))
    route = [(i - distance, i) for i in devices if i - distance in devices]
    return lax.ppermute(block, axis, route)


def band_matrix(filter_taps, out_rows):
    tap_count, group_count = filter_taps.shape
    leading = jnp.flip(filter_taps, 0).T
    padded = jnp.concatenate([leading, jnp.zeros((group_count, out_rows), filter_taps.dtype)], 1)
    span_len = out_rows + tap_count - 1
    tiled_rows = jnp.tile(padded, (1, out_rows))[:, : out_rows * span_len]
    return tiled_rows.reshape(group_count, out_rows, span_len)


def diagonal_sums(cross_terms, tap_count):
    group_count, out_rows, span_len = cross_terms.shape
    flat_view = jnp.pad(
        cross_terms.reshape(group_count, out_rows * span_len), ((0, 0), (0, out_rows))
    )
    skewed = flat_view.reshape(group_count, out_rows, span_len + 1)
    return jnp.flip(jnp.sum(skewed[:, :, :tap_count], axis=1), 1)


def short_features(padded, chan_short, out_rows):
    lag_count = chan_short.shape[1]
    running = jnp.zeros((3, out_rows, padded.shape[1]), jnp.float32)
    for offset in range(lag_count):
        first_row = lag_count - 1 - offset
        running = running + chan_short[:, offset, None, :] * padded[
            None, first_row : first_row + out_rows
        ].astype(jnp.float32)
    return running.astype(jnp.bfloat16)


def medium_block(operands, row_block):
    filter_blk, kv_blk, gate_blk = operands
    tap_count = filter_blk.shape[0]
    seq_rows = gate_blk.shape[0] - tap_count + 1
    span_len = row_block + tap_count - 1
    toeplitz = band_matrix(filter_blk, row_block)

    def row_part(start):
        kv_win = lax.dynamic_slice_in_dim(kv_blk, start, span_len, 0)
        gate_win = lax.dynamic_slice_in_dim(gate_blk, start, span_len, 0)
        gate_rows = gate_win[:row_block]
        mixed_out = jnp.einsum("gts,sgc->tgc", toeplitz, kv_win, preferred_element_type=jnp.float32)
        back_out = jnp.flip(
            jnp.einsum(
                "gts,sgc->tgc", toeplitz, jnp.flip(gate_win, 0), preferred_element_type=jnp.float32
            ),
            0,
        )
        cross_terms = jnp.einsum(
            "tgc,sgc->gts", gate_rows, kv_win, preferred_element_type=jnp.float32
        )
        return (mixed_out, back_out, diagonal_sums(cross_terms, tap_count).T)

    starts = jnp.arange(seq_rows // row_block, dtype=jnp.int32) * row_block
    mixed_out, back_out, taps_grad = lax.map(row_part, starts)
    full_shape = (seq_rows,) + mixed_out.shape[2:]
    return (mixed_out.reshape(full_shape), back_out.reshape(full_shape), jnp.sum(taps_grad, 0))


def split_groups(values_in, block_count, group_width):
    length = values_in.shape[0]
    return values_in.reshape(length, block_count, -1, group_width).transpose(1, 0, 2, 3)


def join_groups(blocks):
    block_count, length, block_groups, group_width = blocks.shape
    return blocks.transpose(1, 0, 2, 3).reshape(length, block_count * block_groups * group_width)


def per_device(inputs, upstream, short_filter, medium_filter):
    signal = inputs[0]
    grad_out = upstream[0]
    seq_rows, chan_count = signal.shape
    tap_count = medium_filter.shape[1]
    group_count = medium_filter.shape[2]
    lag_count = short_filter.shape[1] // 3
    group_width = chan_count // group_count
    short_rim = lag_count - 1
    medium_rim = tap_count - 1
    chan_short = jnp.broadcast_to(
        short_filter[0].astype(jnp.float32).reshape(3, lag_count, group_count, 1),
        (3, lag_count, group_count, group_width),
    ).reshape(3, lag_count, chan_count)
    medium_taps = medium_filter[0]
    zero_rim = jnp.zeros((short_rim, chan_count), jnp.bfloat16)
    features_local = short_features(jnp.concatenate([zero_rim, signal], 0), chan_short, seq_rows)
    kv_local = (
        features_local[1].astype(jnp.float32) * features_local[2].astype(jnp.float32)
    ).astype(jnp.bfloat16)
    signal_rim, kv_rim = passed_along(
        (signal[seq_rows - short_rim :], kv_local[seq_rows - medium_rim :]), "ctx", 1
    )
    signal_pad = jnp.concatenate([signal_rim, signal], 0)
    head_features = short_features(signal_pad[: 2 * short_rim], chan_short, short_rim)
    features = jnp.concatenate([head_features, features_local[:, short_rim:]], 1)
    query_in = features[0]
    key_in = features[1]
    value_in = features[2]
    head_products = (
        key_in[:short_rim].astype(jnp.float32) * value_in[:short_rim].astype(jnp.float32)
    ).astype(jnp.bfloat16)
    products = jnp.concatenate([head_products, kv_local[short_rim:]], 0)
    kv_pad = jnp.concatenate([kv_rim, products], 0)
    gate_grad = (grad_out.astype(jnp.float32) * query_in.astype(jnp.float32)).astype(jnp.bfloat16)
    gate_rim = passed_along(gate_grad[:medium_rim], "ctx", -1)
    gate_ext = jnp.concatenate([gate_grad, gate_rim], 0)
    block_groups = 8
    block_count = group_count // block_groups
    row_block = 128
    taps_blocks = medium_taps.reshape(tap_count, block_count, block_groups).transpose(1, 0, 2)
    mixed_blocks, back_blocks, grad_blocks = lax.map(
        partial(medium_block, row_block=row_block),
        (
            taps_blocks,
            split_groups(kv_pad, block_count, group_width),
            split_groups(gate_ext, block_count, group_width),
        ),
    )
    mixed_out = join_groups(mixed_blocks)
    back_out = join_groups(back_blocks)
    taps_grad = grad_blocks.transpose(1, 0, 2).reshape(tap_count, group_count)
    query_grad = (grad_out.astype(jnp.float32) * mixed_out).astype(jnp.bfloat16)
    key_grad = (back_out * value_in.astype(jnp.float32)).astype(jnp.bfloat16)
    value_grad = (back_out * key_in.astype(jnp.float32)).astype(jnp.bfloat16)
    feature_grads = jnp.stack([query_grad, key_grad, value_grad])
    feature_rim = passed_along(feature_grads[:, :short_rim], "ctx", -1)
    grads_pad = jnp.concatenate([feature_grads, feature_rim], 1)
    running = jnp.zeros((seq_rows, chan_count), jnp.float32)
    short_rows = []
    for offset in range(lag_count):
        running = running + jnp.sum(
            chan_short[:, offset, None, :]
            * grads_pad[:, offset : offset + seq_rows].astype(jnp.float32),
            axis=0,
        )
        lag_start = short_rim - offset
        short_rows.append(
            jnp.sum(
                feature_grads.astype(jnp.float32)
                * signal_pad[None, lag_start : lag_start + seq_rows].astype(jnp.float32),
                axis=1,
            )
        )
    input_grad = running.astype(jnp.bfloat16)
    short_grad = jnp.stack(short_rows, 1).reshape(3 * lag_count, group_count, group_width).sum(-1)
    short_part, medium_part = (
        lax.psum_scatter(short_grad[None], "ctx", scatter_dimension=2, tiled=True),
        lax.psum_scatter(taps_grad[None], "ctx", scatter_dimension=2, tiled=True),
    )
    incoming = passed_along(input_grad[None], "section", -1)
    return (incoming, short_part, medium_part)


def solution(mesh):
    in_specs = (
        P("section", "ctx", "dp"),
        P("section", "ctx", "dp"),
        P("section", None, "dp"),
        P("section", None, "dp"),
    )
    out_specs = (
        P("section", "ctx", "dp"),
        P("section", None, ("dp", "ctx")),
        P("section", None, ("dp", "ctx")),
    )
    return jax.shard_map(
        per_device, mesh=mesh, in_specs=in_specs, out_specs=out_specs, check_vma=False
    )
```

profile of v0, /device:TPU:1, one launch (start us, length us, event | category | flops | bytes accessed | tf_op | source)
XLA Modules:
  0.0 250.4 jit_solution(318119703896194819)
XLA Ops:
  8.0 4.1 %collective-permute-start.1 = (bf16[6,1024]{1,0:T(8,128)(2,1)S(1)}, bf16[6,1024]{1,0:T(8,128)(2,1)S(1)}, u32[]{:S(2)}, u32[]{:S(2)}) collective-permute-start(bf16[6,1024]{1,0:T(8,128)(2,1)S(1)} %get-tuple-element.286), channel_id=1, source_target_pairs={{0,4},{1,5},{2,6},{3,7},{8,12},{9,13},{10,14},{11,15},{16,20},{17,... | collective-permute-start | bytes 36872 | tf_op jit(solution)/shard_map/ppermute | solution.py:12
  14.1 3.1 %fusion.21 = (f32[256,1024]{1,0:T(8,128)}, f32[256,1024]{1,0:T(8,128)}, f32[256,1024]{1,0:T(8,128)}, f32[256,1024]{1,0:T(8,128)}, f32[256,1024]{1,0:T(8,128)}, /...) fusion(bf16[6,1024]{1,0:T(8,128)(2,1)S(1)} %collective-permute-, ...), kind=kLoop, calls=%fused_computation.67 | loop fusion | flops 7864320 | bytes 13119488 | tf_op jit(solution)/shard_map/convert_element_type | solution.py:153
  17.1 1.5 add_convert_fusion
  22.2 4.0 %collective-permute-start = (bf16[127,1024]{1,0:T(8,128)(2,1)S(1)}, bf16[127,1024]{1,0:T(8,128)(2,1)S(1)}, u32[]{:S(2)}, u32[]{:S(2)}) collective-permute-start(bf16[127,1024]{1,0:T(8,128)(2,1)S(1)} %slice_bitcast_fusion.2), channel_id=1, source_target_pairs={{0,4},{1,5},{2,6},{3,7},{8,12},{9,13},{10,14},{11,15},{16,20},{17,... | collective-permute-start | bytes 780296 | tf_op jit(solution)/shard_map/ppermute | solution.py:12
  26.2 3.2 %collective-permute-done.2 = bf16[127,1024]{1,0:T(8,128)(2,1)S(1)} collective-permute-done((bf16[127,1024]{1,0:T(8,128)(2,1)S(1)}, bf16[127,1024]{1,0:T(8,128)(2,1)S(1)}, u32[]{:S(2)}, u32[]{:S(2)}) %collective-permute-start.2) | collective-permute-done | bytes 260128 | tf_op jit(solution)/shard_map/ppermute | solution.py:12
  32.0 163.3 %while.46 = (s32[]{:T(128)}, f32[8,256,8,16]{1,3,2,0:T(8,128)}, f32[8,256,8,16]{1,3,2,0:T(8,128)}, f32[8,128,8]{1,2,0:T(8,128)}, bf16[8,383,8,16]{1,3,2,0:T(8,12...) while((s32[]{:T(128)}, f32[8,256,8,16]{1,3,2,0:T(8,128)}, ...), condition=%wide.region_5.6_spmd, body=%wide.region_0.5_spmd.sunk | while | flops 25198600 | bytes 11929030 | solution.py:124
  33.8 1.4 reshape.190
  35.2 15.0 %while.47 = (s32[]{:T(128)}, f32[2,128,8,16]{1,0,3,2:T(2,128)S(1)}, f32[2,128,8,16]{1,0,3,2:T(2,128)S(1)}, f32[2,128,8]{1,2,0:T(8,128)S(1)}, s32[2]{0:T(128)S(1)...) while((s32[]{:T(128)}, f32[2,128,8,16]{1,0,3,2:T(2,128)S(1)}, ...), condition=%wide.region_3.3_spmd, body=%wide.region_1.2_spmd.sunk | while | flops 25197572 | bytes 7834299 | solution.py:68
  41.4 1.4 dynamic_update_slice.54
  48.9 1.4 dynamic_update_slice.54
  54.2 1.4 reshape.190
  55.7 15.0 %while.47 = (s32[]{:T(128)}, f32[2,128,8,16]{1,0,3,2:T(2,128)S(1)}, f32[2,128,8,16]{1,0,3,2:T(2,128)S(1)}, f32[2,128,8]{1,2,0:T(8,128)S(1)}, s32[2]{0:T(128)S(1)...) while((s32[]{:T(128)}, f32[2,128,8,16]{1,0,3,2:T(2,128)S(1)}, ...), condition=%wide.region_3.3_spmd, body=%wide.region_1.2_spmd.sunk | while | flops 25197572 | bytes 7834299 | solution.py:68
  61.8 1.4 dynamic_update_slice.54
  69.3 1.4 dynamic_update_slice.54
  74.7 1.4 reshape.190
  76.1 15.0 %while.47 = (s32[]{:T(128)}, f32[2,128,8,16]{1,0,3,2:T(2,128)S(1)}, f32[2,128,8,16]{1,0,3,2:T(2,128)S(1)}, f32[2,128,8]{1,2,0:T(8,128)S(1)}, s32[2]{0:T(128)S(1)...) while((s32[]{:T(128)}, f32[2,128,8,16]{1,0,3,2:T(2,128)S(1)}, ...), condition=%wide.region_3.3_spmd, body=%wide.region_1.2_spmd.sunk | while | flops 25197572 | bytes 7834299 | solution.py:68
  82.2 1.4 dynamic_update_slice.54
  89.7 1.4 dynamic_update_slice.54
  95.1 1.4 reshape.190
  96.5 15.0 %while.47 = (s32[]{:T(128)}, f32[2,128,8,16]{1,0,3,2:T(2,128)S(1)}, f32[2,128,8,16]{1,0,3,2:T(2,128)S(1)}, f32[2,128,8]{1,2,0:T(8,128)S(1)}, s32[2]{0:T(128)S(1)...) while((s32[]{:T(128)}, f32[2,128,8,16]{1,0,3,2:T(2,128)S(1)}, ...), condition=%wide.region_3.3_spmd, body=%wide.region_1.2_spmd.sunk | while | flops 25197572 | bytes 7834299 | solution.py:68
  102.6 1.4 dynamic_update_slice.54
  110.1 1.4 dynamic_update_slice.54
  115.5 1.4 reshape.190
  116.9 15.0 %while.47 = (s32[]{:T(128)}, f32[2,128,8,16]{1,0,3,2:T(2,128)S(1)}, f32[2,128,8,16]{1,0,3,2:T(2,128)S(1)}, f32[2,128,8]{1,2,0:T(8,128)S(1)}, s32[2]{0:T(128)S(1)...) while((s32[]{:T(128)}, f32[2,128,8,16]{1,0,3,2:T(2,128)S(1)}, ...), condition=%wide.region_3.3_spmd, body=%wide.region_1.2_spmd.sunk | while | flops 25197572 | bytes 7834299 | solution.py:68
  123.1 1.4 dynamic_update_slice.54
  130.6 1.4 dynamic_update_slice.54
  135.9 1.4 reshape.190
  137.3 15.0 %while.47 = (s32[]{:T(128)}, f32[2,128,8,16]{1,0,3,2:T(2,128)S(1)}, f32[2,128,8,16]{1,0,3,2:T(2,128)S(1)}, f32[2,128,8]{1,2,0:T(8,128)S(1)}, s32[2]{0:T(128)S(1)...) while((s32[]{:T(128)}, f32[2,128,8,16]{1,0,3,2:T(2,128)S(1)}, ...), condition=%wide.region_3.3_spmd, body=%wide.region_1.2_spmd.sunk | while | flops 25197572 | bytes 7834299 | solution.py:68
  143.5 1.4 dynamic_update_slice.54
  151.0 1.4 dynamic_update_slice.54
  156.3 1.4 reshape.190
  157.7 15.0 %while.47 = (s32[]{:T(128)}, f32[2,128,8,16]{1,0,3,2:T(2,128)S(1)}, f32[2,128,8,16]{1,0,3,2:T(2,128)S(1)}, f32[2,128,8]{1,2,0:T(8,128)S(1)}, s32[2]{0:T(128)S(1)...) while((s32[]{:T(128)}, f32[2,128,8,16]{1,0,3,2:T(2,128)S(1)}, ...), condition=%wide.region_3.3_spmd, body=%wide.region_1.2_spmd.sunk | while | flops 25197572 | bytes 7834299 | solution.py:68
  163.9 1.4 dynamic_update_slice.54
  171.4 1.4 dynamic_update_slice.54
  176.7 1.4 reshape.190
  178.2 15.0 %while.47 = (s32[]{:T(128)}, f32[2,128,8,16]{1,0,3,2:T(2,128)S(1)}, f32[2,128,8,16]{1,0,3,2:T(2,128)S(1)}, f32[2,128,8]{1,2,0:T(8,128)S(1)}, s32[2]{0:T(128)S(1)...) while((s32[]{:T(128)}, f32[2,128,8,16]{1,0,3,2:T(2,128)S(1)}, ...), condition=%wide.region_3.3_spmd, body=%wide.region_1.2_spmd.sunk | while | flops 25197572 | bytes 7834299 | solution.py:68
  184.3 1.4 dynamic_update_slice.54
  191.8 1.4 dynamic_update_slice.54
  195.3 2.7 %copy.27 = f32[1,256,1024]{2,1,0:T(8,128)} copy(f32[1,256,1024]{1,2,0:T(8,128)} %bitcast.128) | data formatting | bytes 2097152 | tf_op jit(solution)/shard_map/reshape | solution.py:80
  198.0 1.6 multiply_convert_fusion.1
  199.6 2.7 %copy.26 = f32[1,256,1024]{2,1,0:T(8,128)} copy(f32[1,256,1024]{1,2,0:T(8,128)} %bitcast.127) | data formatting | bytes 2097152 | tf_op jit(solution)/shard_map/reshape | solution.py:80
  202.3 1.6 fusion.16
  204.2 1.6 collective-permute-start.3
  205.9 2.1 fusion.11
  209.3 3.6 %multiply_reduce_fusion.5 = (f32[256,1024]{1,0:T(8,128)S(1)}, f32[256,1024]{1,0:T(8,128)S(1)}, f32[256,1024]{1,0:T(8,128)S(1)}, f32[256,1024]{1,0:T(8,128)S(1)},...) fusion(bf16[3,262,1024]{2,1,0:T(8,128)(2,1)S(1)} %pad_maximum_fusion, f32[3,1024]{1,0:T(4,128)S(1)} %get-tuple-element.300, ...), kind=kLoop, calls=%fused_computation.39 | loop fusion | flops 12582912 | bytes 15802368 | tf_op jit(solution)/shard_map/reduce_sum | solution.py:144
  213.7 5.1 %collective-permute-start.4 = (bf16[1,256,1024]{2,1,0:T(8,128)(2,1)S(1)}, bf16[1,256,1024]{2,1,0:T(8,128)(2,1)S(1)}, u32[]{:S(2)}, u32[]{:S(2)}) collective-permute-start(bf16[1,256,1024]{2,1,0:T(8,128)(2,1)S(1)} %fusion.17), channel_id=1, source_target_pairs={{8,0},{16,8},{24,16},{9,1},{17,9},{25,17},{10,2},{18,10},{26,18},{... | collective-permute-start | bytes 1572872 | tf_op jit(solution)/shard_map/ppermute | solution.py:12
  221.7 8.5 %reduce-scatter.7.cloned.1.call-done = f32[32,21]{1,0:T(8,128)} async-done(((f32[64,21]{1,0:T(8,128)}), f32[32,21]{1,0:T(8,128)}) %reduce-scatter.7.cloned.1.call-update) | async-done | bytes 2704
  231.9 10.9 %reduce-scatter.5.cloned.1.call-done = f32[1,128,32]{1,2,0:T(8,128)} async-done(((f32[1,128,64]{1,2,0:T(8,128)}), f32[1,128,32]{1,2,0:T(8,128)}) %reduce-scatter.5.cloned.1.call-update) | async-done | bytes 16400 | tf_op jit(solution)/shard_map/reduce_scatter | solution.py:161
  (417 shorter events, 116.4 us)
Async XLA Ops:
  7.2 6.1 %copy-start.12 = (bf16[1,21,64]{2,1,0:T(8,128)(2,1)S(1)}, bf16[1,21,64]{2,1,0:T(8,128)(2,1)}, u32[]{:S(2)}) copy-start(bf16[1,21,64]{2,1,0:T(8,128)(2,1)} %param.10) | copy-start | bytes 8068
  7.2 223.0 %reduce-scatter.7.cloned.1.call-start = ((), (), s32[]{:S(2)}) async-start(), calls=%async_computation.3 | async-start | bytes 49152
  8.0 6.1 %copy-start.4 = (bf16[1,256,1024]{2,1,0:T(8,128)(2,1)S(1)}, bf16[1,256,1024]{2,1,0:T(8,128)(2,1)}, u32[]{:S(2)}) copy-start(bf16[1,256,1024]{2,1,0:T(8,128)(2,1)} %param.8) | copy-start | bytes 1572868
  8.0 6.1 %collective-permute-start.1 = (bf16[6,1024]{1,0:T(8,128)(2,1)S(1)}, bf16[6,1024]{1,0:T(8,128)(2,1)S(1)}, u32[]{:S(2)}, u32[]{:S(2)}) collective-permute-start(bf16[6,1024]{1,0:T(8,128)(2,1)S(1)} %get-tuple-element.286), channel_id=1, source_target_pairs={{0,4},{1,5},{2,6},{3,7},{8,12},{9,13},{10,14},{11,15},{16,20},{17,... | collective-permute-start | bytes 36872 | tf_op jit(solution)/shard_map/ppermute | solution.py:12
  13.3 3.9 %copy-start.2 = (f32[256,1024]{1,0:T(8,128)}, f32[256,1024]{1,0:T(8,128)S(1)}, u32[]{:S(2)}) copy-start(f32[256,1024]{1,0:T(8,128)S(1)} %bitcast_convert_fusion.1) | copy-start | bytes 3145732
  19.0 1.7 copy-start
  19.0 1.4 copy-start.11
  20.7 8.8 %collective-permute-start.2 = (bf16[127,1024]{1,0:T(8,128)(2,1)S(1)}, bf16[127,1024]{1,0:T(8,128)(2,1)S(1)}, u32[]{:S(2)}, u32[]{:S(2)}) collective-permute-start(bf16[127,1024]{1,0:T(8,128)(2,1)S(1)} %slice_bitcast_fusion.1), channel_id=1, source_target_pairs={{4,0},{5,1},{6,2},{7,3},{12,8},{13,9},{14,10},{15,11},{20,16},{21,... | collective-permute-start | bytes 780296 | tf_op jit(solution)/shard_map/ppermute | solution.py:12
  22.2 8.5 %collective-permute-start = (bf16[127,1024]{1,0:T(8,128)(2,1)S(1)}, bf16[127,1024]{1,0:T(8,128)(2,1)S(1)}, u32[]{:S(2)}, u32[]{:S(2)}) collective-permute-start(bf16[127,1024]{1,0:T(8,128)(2,1)S(1)} %slice_bitcast_fusion.2), channel_id=1, source_target_pairs={{0,4},{1,5},{2,6},{3,7},{8,12},{9,13},{10,14},{11,15},{16,20},{17,... | collective-permute-start | bytes 780296 | tf_op jit(solution)/shard_map/ppermute | solution.py:12
  195.3 2.7 %copy-start.1 = (bf16[3,250,1024]{2,1,0:T(8,128)(2,1)S(1)}, bf16[3,250,1024]{2,1,0:T(8,128)(2,1)}, u32[]{:S(2)}) copy-start(bf16[3,250,1024]{2,1,0:T(8,128)(2,1)} %copy-done) | copy-start | bytes 4608004
  199.6 6.2 %copy-start.9 = (f32[256,1024]{1,0:T(8,128)S(1)}, f32[256,1024]{1,0:T(8,128)}, u32[]{:S(2)}) copy-start(f32[256,1024]{1,0:T(8,128)} %get-tuple-element.272) | copy-start | bytes 3145732
  199.6 6.2 %copy-start.10 = (f32[256,1024]{1,0:T(8,128)S(1)}, f32[256,1024]{1,0:T(8,128)}, u32[]{:S(2)}) copy-start(f32[256,1024]{1,0:T(8,128)} %get-tuple-element.273) | copy-start | bytes 3145732
  202.3 3.5 %copy-start.7 = (f32[256,1024]{1,0:T(8,128)S(1)}, f32[256,1024]{1,0:T(8,128)}, u32[]{:S(2)}) copy-start(f32[256,1024]{1,0:T(8,128)} %get-tuple-element.270) | copy-start | bytes 3145732
  202.3 3.5 %copy-start.8 = (f32[256,1024]{1,0:T(8,128)S(1)}, f32[256,1024]{1,0:T(8,128)}, u32[]{:S(2)}) copy-start(f32[256,1024]{1,0:T(8,128)} %get-tuple-element.271) | copy-start | bytes 3145732
  204.0 1.9 copy-start.3
  204.0 1.9 copy-start.5
  204.0 1.9 copy-start.6
  204.2 5.0 %collective-permute-start.3 = (bf16[3,6,1024]{2,1,0:T(8,128)(2,1)S(1)}, bf16[3,6,1024]{2,1,0:T(8,128)(2,1)S(1)}, u32[]{:S(2)}, u32[]{:S(2)}) collective-permute-start(bf16[3,6,1024]{2,1,0:T(8,128)(2,1)S(1)} %slice.262), channel_id=1, source_target_pairs={{4,0},{5,1},{6,2},{7,3},{12,8},{13,9},{14,10},{15,11},{20,16},{21,... | collective-permute-start | bytes 110600 | tf_op jit(solution)/shard_map/ppermute | solution.py:12
  213.7 18.1 %collective-permute-start.4 = (bf16[1,256,1024]{2,1,0:T(8,128)(2,1)S(1)}, bf16[1,256,1024]{2,1,0:T(8,128)(2,1)S(1)}, u32[]{:S(2)}, u32[]{:S(2)}) collective-permute-start(bf16[1,256,1024]{2,1,0:T(8,128)(2,1)S(1)} %fusion.17), channel_id=1, source_target_pairs={{8,0},{16,8},{24,16},{9,1},{17,9},{25,17},{10,2},{18,10},{26,18},{... | collective-permute-start | bytes 1572872 | tf_op jit(solution)/shard_map/ppermute | solution.py:12
  220.9 21.9 %reduce-scatter.5.cloned.1.call-start = ((), (), s32[]{:S(2)}) async-start(), calls=%async_computation.2 | async-start | bytes 49152 | tf_op jit(solution)/shard_map/reduce_scatter | solution.py:161
Sparse Core Ops, SparseCore 0:
  221.0 9.1 reduce-scatter.6
  233.0 9.8 reduce-scatter.4
where the time goes:
time: 253 us; the launch traced here: 250 us
  local copies, waits for them, and re-layouts  129 us (51%)
  loops' own time  30.7 us (12%)
  waiting for transfers between devices  24.5 us (10%)
  other arithmetic  19.7 us (8%)
  starting transfers between devices  16.2 us (6%)
  matrix products  16 us (6%)
  between operations  14.6 us (6%)
    dynamic_update_slice x48, local copies, waits for them, and re-layouts, medium_block(): mixed_out, back_out, taps_grad = lax.map(row_part, starts)  43.1 us
    another operation x8, loops' own time, medium_block(): mixed_out, back_out, taps_grad = lax.map(row_part, starts)  30.1 us
    ppermute x5, starting transfers between devices, passed_along(): return lax.ppermute(block, axis, route)  16.1 us
    dynamic_update_slice x24, local copies, waits for them, and re-layouts, per_device(): lax.map(partial(medium_block, row_block=row_block), (taps_blocks, split_g...  15.4 us
    squeeze x16, local copies, waits for them, and re-layouts, per_device(): lax.map(partial(medium_block, row_block=row_block), (taps_blocks, split_g...  13.2 us
    reshape x8, local copies, waits for them, and re-layouts, band_matrix(): return tiled_rows.reshape(group_count, out_rows, span_len)  10.9 us
    reduce_scatter x1, waiting for transfers between devices, per_device(): lax.psum_scatter(taps_grad[None], 'ctx', scatter_dimension=2, tiled=True)  10.9 us
    dynamic_slice x16, local copies, waits for them, and re-layouts, medium_block(): mixed_out, back_out, taps_grad = lax.map(row_part, starts)  9.83 us
  transfers between devices with their start and end apart: 7, of which 4 were waited for; matrix products, arithmetic and copies ran while one was open for 4% of the time, Pallas kernels for 0%

commit v1 on v0

v1 whole, which is shorter than its diff:
```python
from functools import partial

import jax
import jax.numpy as jnp
from jax import lax
from jax.experimental import pallas as pl
from jax.experimental.pallas import tpu as pltpu
from jax.sharding import PartitionSpec as P

MESH = pl.DeviceIdType.MESH
F32 = jnp.float32
BF16 = jnp.bfloat16
LANES = 128
RIM = 8
CHUNK = 64


def iota(shape, dim):
    return lax.broadcasted_iota(jnp.int32, shape, dim)


def kernel(
    dims,
    x_ref, gy_ref, sf_ref, mf_ref,
    out_ref, gs_ref, gm_ref,
    hf, hb, wsc, tm, tk, xf, xrim, kvp, gext, keyb, valb, ef, ot, zb, grads, snd, rcv, tr,
    bx_s, bx_r, kv_s, kv_r, ga_s, ga_r, er_s, er_r, ou_s, ou_r, gr_s, gr_r, z_sem,
):
    n_ctx, n_sec, rows, tiles, lags, taps, width = dims
    c = lax.axis_index("ctx")
    s = lax.axis_index("section")
    nxt = lax.rem(c + 1, n_ctx)
    prv = lax.rem(c + n_ctx - 1, n_ctx)
    has_next = c < n_ctx - 1
    has_prev = c > 0
    sends_out = s > 0
    gets_out = s < n_sec - 1
    down = lax.rem(s + n_sec - 1, n_sec)
    up = lax.rem(s + 1, n_sec)
    gpt = LANES // width
    groups = gpt * tiles
    gpd = groups // n_ctx
    nb = rows // taps
    span = 2 * taps
    features = 3

    barrier = pltpu.get_barrier_semaphore()
    for d in range(1, n_ctx):
        pl.semaphore_signal(
            barrier, inc=1, device_id={"ctx": lax.rem(c + d, n_ctx)}, device_id_type=MESH
        )

    @pl.when(sends_out)
    def _():
        pl.semaphore_signal(barrier, inc=1, device_id={"section": down}, device_id_type=MESH)

    @pl.when(gets_out)
    def _():
        pl.semaphore_signal(barrier, inc=1, device_id={"section": up}, device_id_type=MESH)

    def remote(src, dst, send, recv, where):
        return pltpu.make_async_remote_copy(
            src_ref=src, dst_ref=dst, send_sem=send, recv_sem=recv,
            device_id=where, device_id_type=MESH,
        )

    def x_copy():
        return remote(
            x_ref.at[0, pl.ds(rows - 16, 16)], xrim, bx_s.at[0], bx_r.at[0], {"ctx": nxt}
        )

    def kv_copy(k):
        return remote(
            kvp.at[k, pl.ds(rows, taps)], kvp.at[k, pl.ds(0, taps)],
            kv_s.at[k], kv_r.at[k], {"ctx": nxt},
        )

    def gate_copy(k):
        return remote(
            gext.at[k, pl.ds(0, taps)], gext.at[k, pl.ds(rows, taps)],
            ga_s.at[k], ga_r.at[k], {"ctx": prv},
        )

    def rim_copy(k):
        return remote(
            ef.at[k, :, pl.ds(0, RIM)], ef.at[k, :, pl.ds(rows, RIM)],
            er_s.at[k], er_r.at[k], {"ctx": prv},
        )

    def out_copy(k):
        return remote(
            ot.at[k], out_ref.at[0, :, pl.ds(pl.multiple_of(k * LANES, LANES), LANES)],
            ou_s.at[k], ou_r.at[k], {"section": down},
        )

    taps_in = mf_ref[0]
    dot_tn = partial(
        lax.dot_general, dimension_numbers=(((0,), (0,)), ((), ())), preferred_element_type=F32
    )
    dot_nt = partial(
        lax.dot_general, dimension_numbers=(((1,), (1,)), ((), ())), preferred_element_type=F32
    )
    row_j, col_m = iota((taps, span), 0), iota((taps, span), 1)
    flipped = dot_tn(taps_in, (col_m == taps - row_j).astype(BF16))
    straight = dot_tn(taps_in, (col_m == row_j).astype(BF16))
    spread = (iota((groups, tiles * LANES), 1) // width == iota((groups, tiles * LANES), 0))
    wide = jnp.dot(sf_ref[0], spread.astype(BF16), preferred_element_type=F32)
    for k in range(tiles):
        hf[k] = flipped[k * gpt : (k + 1) * gpt]
        hb[k] = straight[k * gpt : (k + 1) * gpt]
        wsc[k, 0 : features * lags] = wide[:, k * LANES : (k + 1) * LANES]

    def build(k, carry):
        for u in range(gpt):
            for rows_of, dest in ((hf, tm), (hb, tk)):
                line = jnp.broadcast_to(rows_of[k, u : u + 1], (taps, span))
                band = pltpu.roll(line, 0, 1, stride=1, stride_axis=0)
                dest[k, :, u * span : (u + 1) * span] = band.astype(BF16)
        return carry

    lax.fori_loop(0, tiles // 2, build, 0)

    pl.semaphore_wait(
        barrier, n_ctx - 1 + sends_out.astype(jnp.int32) + gets_out.astype(jnp.int32)
    )

    @pl.when(has_next)
    def _():
        x_copy().start()

    @pl.when(jnp.logical_not(has_prev))
    def _():
        xrim[...] = jnp.zeros_like(xrim)
        kvp[:, 0:taps] = jnp.zeros((tiles, taps, LANES), BF16)

    @pl.when(jnp.logical_not(has_next))
    def _():
        gext[:, rows : rows + taps] = jnp.zeros((tiles, taps, LANES), BF16)
        ef[:, :, rows : rows + RIM] = jnp.zeros((tiles, features, RIM, LANES), F32)

    def zero_copy():
        return pltpu.make_async_copy(zb, out_ref.at[0], z_sem.at[0])

    @pl.when(jnp.logical_not(gets_out))
    def _():
        zb[...] = jnp.zeros_like(zb)
        zero_copy().start()

    lax.fori_loop(tiles // 2, tiles, build, 0)

    @pl.when(has_prev)
    def _():
        x_copy().wait_recv()

    def lane_slice(k):
        return pl.ds(pl.multiple_of(k * LANES, LANES), LANES)

    def feature_tile(k, carry):
        xf[k, RIM : RIM + rows] = x_ref[0, :, lane_slice(k)].astype(F32)
        xf[k, 0:RIM] = xrim[:, lane_slice(k)].astype(F32)[16 - RIM :]
        for start in range(0, rows, CHUNK):
            sums = [jnp.zeros((CHUNK, LANES), F32) for _ in range(features)]
            for i in range(lags):
                window = xf[k, RIM + start - i : RIM + start - i + CHUNK]
                for f in range(features):
                    sums[f] = sums[f] + wsc[k, f * lags + i : f * lags + i + 1] * window
            q, key, val = [v.astype(BF16) for v in sums]
            here = slice(start, start + CHUNK)
            keyb[k, here] = key
            valb[k, here] = val
            kvp[k, taps + start : taps + start + CHUNK] = (
                key.astype(F32) * val.astype(F32)
            ).astype(BF16)
            gext[k, here] = (
                gy_ref[0, here, lane_slice(k)].astype(F32) * q.astype(F32)
            ).astype(BF16)

        @pl.when(has_next)
        def _():
            kv_copy(k).start()

        @pl.when(has_prev)
        def _():
            gate_copy(k).start()

        return carry

    lax.fori_loop(0, tiles, feature_tile, 0)

    lane_group = lax.rem(iota((1, nb * LANES), 1), LANES) // width
    masks = [(lane_group == u).astype(BF16) for u in range(gpt)]
    reverse = (iota((taps, taps), 0) + iota((taps, taps), 1) == taps - 1).astype(BF16)

    def windows(ref, k):
        return jnp.concatenate(
            [ref[k, b * taps : b * taps + span] for b in range(nb)], axis=1
        )

    def medium_tile(k):
        @pl.when(has_prev)
        def _():
            kv_copy(k).wait_recv()

        @pl.when(has_next)
        def _():
            gate_copy(k).wait_recv()

        kv_win = windows(kvp, k)
        gate_win = windows(gext, k)
        mixed = jnp.zeros((taps, nb * LANES), F32)
        back = jnp.zeros((taps, nb * LANES), F32)
        for u in range(gpt):
            cols = slice(u * span, (u + 1) * span)
            mixed = mixed + jnp.dot(
                tm[k, :, cols], kv_win * masks[u], preferred_element_type=F32
            )
            back = back + jnp.dot(
                tk[k, :, cols], gate_win * masks[u], preferred_element_type=F32
            )
        for b in range(nb):
            here = slice(b * taps, (b + 1) * taps)
            mix_b = mixed[:, b * LANES : (b + 1) * LANES]
            back_b = back[:, b * LANES : (b + 1) * LANES]
            ef[k, 0, here] = (
                gy_ref[0, here, lane_slice(k)].astype(F32) * mix_b
            ).astype(BF16).astype(F32)
            ef[k, 1, here] = (back_b * valb[k, here].astype(F32)).astype(BF16).astype(F32)
            ef[k, 2, here] = (back_b * keyb[k, here].astype(F32)).astype(BF16).astype(F32)

        @pl.when(has_prev)
        def _():
            rim_copy(k).start()

        kv_own = jnp.concatenate(
            [kvp[k, taps + b * taps : span + b * taps] for b in range(nb)], axis=1
        )
        kv_rev = jnp.dot(reverse, kv_own, preferred_element_type=F32).astype(BF16)
        lines = []
        for u in range(gpt):
            cross = dot_nt(kv_rev * masks[u], gate_win)
            turned = pltpu.roll(cross, 0, 1, stride=1, stride_axis=0)
            lines.append(jnp.sum(turned, axis=0, keepdims=True))
        diag = pltpu.roll(jnp.concatenate(lines, axis=0), span - taps + 1, 1)
        grads[pl.ds(pl.multiple_of(k * gpt, gpt), gpt), 0:taps] = diag[:, 0:taps]

    gather = (iota((gpt, LANES), 1) // width == iota((gpt, LANES), 0)).astype(F32)

    def short_tile(k):
        @pl.when(has_next)
        def _():
            rim_copy(k).wait_recv()

        sums = [jnp.zeros((8, LANES), F32) for _ in range(features * lags)]
        for start in range(0, rows, CHUNK):
            x_here = xf[k, RIM + start : RIM + start + CHUNK]
            total = jnp.zeros((CHUNK, LANES), F32)
            for f in range(features):
                for i in range(lags):
                    at = f * lags + i
                    e = ef[k, f, start + i : start + i + CHUNK]
                    total = total + wsc[k, at : at + 1] * e
                    sums[at] = sums[at] + jnp.sum(
                        (e * x_here).reshape(CHUNK // 8, 8, LANES), axis=0
                    )
            ot[k, start : start + CHUNK] = total.astype(BF16)

        @pl.when(sends_out)
        def _():
            out_copy(k).start()

        flat = [jnp.sum(v, axis=0, keepdims=True) for v in sums]
        flat.append(jnp.zeros((LANES - features * lags, LANES), F32))
        flat = jnp.concatenate(flat, axis=0)
        grads[pl.ds(pl.multiple_of(k * gpt, gpt), gpt), taps : taps + LANES] = dot_nt(
            gather, flat, precision=lax.Precision.HIGHEST
        )

    lag = 2

    def step(k, carry):
        @pl.when(k < tiles)
        def _():
            medium_tile(k)

        @pl.when(k >= lag)
        def _():
            short_tile(k - lag)

        return carry

    lax.fori_loop(0, tiles + lag, step, 0)

    for p in range(n_ctx):
        snd[p] = grads[p * gpd : (p + 1) * gpd]

    def grad_copy(d):
        to = lax.rem(c + d, n_ctx)
        return remote(snd.at[to], rcv.at[d - 1], gr_s.at[d - 1], gr_r.at[d - 1], {"ctx": to})

    for d in range(1, n_ctx):
        grad_copy(d).start()
    total = snd[c]
    for d in range(1, n_ctx):
        grad_copy(d).wait_recv()
        total = total + rcv[d - 1]
    tr[...] = jnp.zeros_like(tr)
    tr[0:gpd] = total
    gm_ref[0] = tr[:, 0:taps].T[:, 0:gpd]
    gs_ref[0] = tr[:, taps : taps + LANES].T[0 : features * lags, 0:gpd]

    for d in range(1, n_ctx):
        grad_copy(d).wait_send()

    @pl.when(has_next)
    def _():
        x_copy().wait_send()

    def drain(k, carry):
        @pl.when(has_next)
        def _():
            kv_copy(k).wait_send()

        @pl.when(has_prev)
        def _():
            gate_copy(k).wait_send()
            rim_copy(k).wait_send()

        @pl.when(sends_out)
        def _():
            out_copy(k).wait_send()

        @pl.when(gets_out)
        def _():
            out_copy(k).wait_recv()

        return carry

    lax.fori_loop(0, tiles, drain, 0)

    @pl.when(jnp.logical_not(gets_out))
    def _():
        zero_copy().wait()


def per_device(n_ctx, n_sec, inputs, upstream, short_filter, medium_filter):
    _, rows, chans = inputs.shape
    taps, groups = medium_filter.shape[1:]
    lags = short_filter.shape[1] // 3
    width = chans // groups
    tiles = chans // LANES
    gpt = LANES // width
    gpd = groups // n_ctx
    dims = (n_ctx, n_sec, rows, tiles, lags, taps, width)
    vmem = pl.BlockSpec(memory_space=pltpu.VMEM)
    dma = pltpu.SemaphoreType.DMA
    span = 2 * taps
    return pl.pallas_call(
        partial(kernel, dims),
        out_shape=(
            jax.ShapeDtypeStruct(inputs.shape, BF16),
            jax.ShapeDtypeStruct((1, 3 * lags, gpd), F32),
            jax.ShapeDtypeStruct((1, taps, gpd), F32),
        ),
        in_specs=[vmem] * 4,
        out_specs=(pl.BlockSpec(memory_space=pl.ANY), vmem, vmem),
        scratch_shapes=[
            pltpu.VMEM((tiles, gpt, span), F32),
            pltpu.VMEM((tiles, gpt, span), F32),
            pltpu.VMEM((tiles, 24, LANES), F32),
            pltpu.VMEM((tiles, taps, gpt * span), BF16),
            pltpu.VMEM((tiles, taps, gpt * span), BF16),
            pltpu.VMEM((tiles, rows + RIM, LANES), F32),
            pltpu.VMEM((16, chans), BF16),
            pltpu.VMEM((tiles, rows + taps, LANES), BF16),
            pltpu.VMEM((tiles, rows + taps, LANES), BF16),
            pltpu.VMEM((tiles, rows, LANES), BF16),
            pltpu.VMEM((tiles, rows, LANES), BF16),
            pltpu.VMEM((tiles, 3, rows + RIM, LANES), F32),
            pltpu.VMEM((tiles, rows, LANES), BF16),
            pltpu.VMEM((rows, chans), BF16),
            pltpu.VMEM((groups, taps + LANES), F32),
            pltpu.VMEM((n_ctx, gpd, taps + LANES), F32),
            pltpu.VMEM((max(n_ctx - 1, 1), gpd, taps + LANES), F32),
            pltpu.VMEM((LANES, taps + LANES), F32),
            dma((1,)), dma((1,)),
            dma((tiles,)), dma((tiles,)),
            dma((tiles,)), dma((tiles,)),
            dma((tiles,)), dma((tiles,)),
            dma((tiles,)), dma((tiles,)),
            dma((max(n_ctx - 1, 1),)), dma((max(n_ctx - 1, 1),)),
            dma((1,)),
        ],
        compiler_params=pltpu.CompilerParams(
            collective_id=0, has_side_effects=True, vmem_limit_bytes=40 * 1024 * 1024
        ),
    )(inputs, upstream, short_filter, medium_filter)


def solution(mesh):
    in_specs = (
        P("section", "ctx", "dp"),
        P("section", "ctx", "dp"),
        P("section", None, "dp"),
        P("section", None, "dp"),
    )
    out_specs = (
        P("section", "ctx", "dp"),
        P("section", None, ("dp", "ctx")),
        P("section", None, ("dp", "ctx")),
    )
    return jax.shard_map(
        partial(per_device, mesh.shape["ctx"], mesh.shape["section"]),
        mesh=mesh, in_specs=in_specs, out_specs=out_specs, check_vma=False,
    )
```

time: 253 us -> 33.1 us (0.13)
  local copies, waits for them, and re-layouts: 129 us -> 5 us
  loops' own time: 30.7 us -> 0 us
  Pallas kernels: 0 us -> 27.2 us
  waiting for transfers between devices: 24.5 us -> 0 us
  other arithmetic: 19.7 us -> 0 us
  starting transfers between devices: 16.2 us -> 0 us
  matrix products: 16 us -> 0 us
  between operations: 14.6 us -> 0.67 us
    dynamic_update_slice x72 -> x0, local copies, waits for them, and re-layouts: 58.5 us -> none  [the longest x48 43.1 us: medium_block(): mixed_out, back_out, taps_grad = lax.map(row_part, starts)]
    another operation x9 -> x0, loops' own time: 30.7 us -> none  [the longest x8 30.1 us: medium_block(): mixed_out, back_out, taps_grad = lax.map(row_part, starts)]
    pallas_call x0 -> x1, Pallas kernels: none -> 27.2 us  [per_device(): pl.pallas_call(partial(kernel, dims), out_shape=(jax.ShapeDtypeStruct(inp...]
    reshape x28 -> x0, local copies, waits for them, and re-layouts: 26.6 us -> none  [the longest x8 10.9 us: band_matrix(): return tiled_rows.reshape(group_count, out_rows, span_len)]
    ppermute x5 -> x0, starting transfers between devices: 16.1 us -> none  [passed_along(): return lax.ppermute(block, axis, route)]
    dot_general x48 -> x0, matrix products: 16 us -> none  [the longest x16 7.53 us: row_part(): jnp.einsum('tgc,sgc->gts', gate_rows, kv_win, preferred_element_type=jnp....]
    squeeze x16 -> x0, local copies, waits for them, and re-layouts: 13.2 us -> none  [per_device(): lax.map(partial(medium_block, row_block=row_block), (taps_blocks, split_g...]
    dynamic_slice x32 -> x0, local copies, waits for them, and re-layouts: 11.3 us -> none  [the longest x16 9.83 us: medium_block(): mixed_out, back_out, taps_grad = lax.map(row_part, starts)]
  transfers between devices with their start and end apart: 7 -> 0, of which waited for: 4 -> 0; matrix products, arithmetic and copies ran while one was open for 4% -> 0% of each run, Pallas kernels for 0% -> 0%
where the time goes in v1:
time: 33.1 us; the launch traced here: 32.8 us
  Pallas kernels  27.2 us (82%)
  local copies, waits for them, and re-layouts  5 us (15%)
  between operations  0.67 us (2%)
    pallas_call x1, Pallas kernels, per_device(): pl.pallas_call(partial(kernel, dims), out_shape=(jax.ShapeDtypeStruct(inp...  27.2 us
    unnamed x8, local copies, waits for them, and re-layouts  3.71 us
    pallas_call x2, local copies, waits for them, and re-layouts, per_device(): pl.pallas_call(partial(kernel, dims), out_shape=(jax.ShapeDtypeStruct(inp...  1.29 us

profile of v1, /device:TPU:1, one launch (start us, length us, event | category | flops | bytes accessed | tf_op | source)
XLA Modules:
  0.0 32.8 jit_solution(13460994515307763600)
XLA Ops:
  0.6 0.0 copy-start.2
  0.6 0.8 %copy.7.mf_ref = bf16[1,128,64]{2,1,0:T(8,128)(2,1)S(1)} copy(bf16[1,128,64]{1,2,0:T(8,128)(2,1)} %param.7) | data formatting | bytes 32768 | tf_op args[3]
  1.5 0.0 copy-done.2
  1.5 0.0 copy-start
  1.5 1.0 %copy-done = bf16[1,256,1024]{2,1,0:T(8,128)(2,1)S(1)} copy-done((bf16[1,256,1024]{2,1,0:T(8,128)(2,1)S(1)}, bf16[1,256,1024]{2,1,0:T(8,128)(2,1)}, u32[]{:S(2)}) %copy-start) | copy-done | bytes 524312
  2.5 0.0 copy-start.1
  2.5 1.0 %copy-done.1 = bf16[1,256,1024]{2,1,0:T(8,128)(2,1)S(1)} copy-done((bf16[1,256,1024]{2,1,0:T(8,128)(2,1)S(1)}, bf16[1,256,1024]{2,1,0:T(8,128)(2,1)}, u32[]{:S(2)}) %copy-start.1) | copy-done | bytes 524312
  3.6 27.2 %shard_map.67 = (bf16[1,256,1024]{2,1,0:T(8,128)(2,1)S(1)}, f32[1,21,32]{2,1,0:T(8,128)S(1)}, f32[1,128,32]{2,1,0:T(8,128)S(1)}) custom-call(bf16[1,256,1024]{2,1,0:T(8,128)(2,1)S(1)} %copy-done, bf16[1,256,1024]{2,1,0:T(8,128)(2,1)S(1)} %copy-done.1, bf16[1,21,64]{2,1,0:T(8,128)(2,1)S(1)} %copy-done.2, bf16[1,128,64]{2,1,0:T(8,128)(2,1)S(1)} %copy.7.mf_ref), custom_call_target="tpu_custom_call" | custom-call | tf_op jit(solution)/shard_map/pallas_call | solution.py:357
  30.8 0.6 %copy.8 = f32[1,21,32]{2,0,1:T(1,128)} copy(f32[1,21,32]{2,1,0:T(8,128)S(1)} %get-tuple-element.4) | data formatting | bytes 5376 | tf_op jit(solution)/shard_map/pallas_call | solution.py:357
  31.4 0.7 %copy.9 = f32[1,128,32]{1,2,0:T(8,128)} copy(f32[1,128,32]{2,1,0:T(8,128)S(1)} %get-tuple-element.5) | data formatting | bytes 32768 | tf_op jit(solution)/shard_map/pallas_call | solution.py:357
  32.0 0.8 %copy.11 = bf16[1,256,1024]{2,1,0:T(8,128)(2,1)} copy(bf16[1,256,1024]{2,1,0:T(8,128)(2,1)S(1)} %get-tuple-element.9) | data formatting | bytes 1048576
Async XLA Ops:
  0.6 0.8 %copy-start.2 = (bf16[1,21,64]{2,1,0:T(8,128)(2,1)S(1)}, bf16[1,21,64]{2,1,0:T(8,128)(2,1)}, u32[]{:S(2)}) copy-start(bf16[1,21,64]{2,1,0:T(8,128)(2,1)} %sf_ref.1) | copy-start | bytes 8068
  1.5 1.0 %copy-start = (bf16[1,256,1024]{2,1,0:T(8,128)(2,1)S(1)}, bf16[1,256,1024]{2,1,0:T(8,128)(2,1)}, u32[]{:S(2)}) copy-start(bf16[1,256,1024]{2,1,0:T(8,128)(2,1)} %x_ref.1) | copy-start | bytes 1572868
  2.5 1.0 %copy-start.1 = (bf16[1,256,1024]{2,1,0:T(8,128)(2,1)S(1)}, bf16[1,256,1024]{2,1,0:T(8,128)(2,1)}, u32[]{:S(2)}) copy-start(bf16[1,256,1024]{2,1,0:T(8,128)(2,1)} %gy_ref.1) | copy-start | bytes 1572868

commit v2 on v1

--- a/solution.py
+++ b/solution.py
@@ -23,8 +23,8 @@
     dims,
     x_ref, gy_ref, sf_ref, mf_ref,
     out_ref, gs_ref, gm_ref,
-    hf, hb, wsc, tm, tk, xf, xrim, kvp, gext, keyb, valb, ef, ot, zb, grads, snd, rcv, tr,
-    bx_s, bx_r, kv_s, kv_r, ga_s, ga_r, er_s, er_r, ou_s, ou_r, gr_s, gr_r, z_sem,
+    xv, gyv, hf, hb, wsc, tm, tk, xf, xrim, kvp, gext, keyb, valb, ef, ot, zb, grads_m, grads_s, snd, rcv, tr,
+    bx_s, bx_r, kv_s, kv_r, ga_s, ga_r, er_s, er_r, ou_s, ou_r, gr_s, gr_r, z_sem, in_sem,
 ):
     n_ctx, n_sec, rows, tiles, lags, taps, width = dims
     c = lax.axis_index("ctx")
@@ -44,6 +44,15 @@
     span = 2 * taps
     features = 3
 
+    def load_x():
+        return pltpu.make_async_copy(x_ref.at[0], xv, in_sem.at[0])
+
+    def load_gy():
+        return pltpu.make_async_copy(gy_ref.at[0], gyv, in_sem.at[1])
+
+    load_x().start()
+    load_gy().start()
+
     barrier = pltpu.get_barrier_semaphore()
     for d in range(1, n_ctx):
         pl.semaphore_signal(
@@ -89,20 +98,19 @@
 
     def out_copy(k):
         return remote(
-            ot.at[k], out_ref.at[0, :, pl.ds(pl.multiple_of(k * LANES, LANES), LANES)],
+            ot.at[k], out_ref.at[k],
             ou_s.at[k], ou_r.at[k], {"section": down},
         )
 
     taps_in = mf_ref[0]
-    dot_tn = partial(
-        lax.dot_general, dimension_numbers=(((0,), (0,)), ((), ())), preferred_element_type=F32
-    )
     dot_nt = partial(
         lax.dot_general, dimension_numbers=(((1,), (1,)), ((), ())), preferred_element_type=F32
     )
     row_j, col_m = iota((taps, span), 0), iota((taps, span), 1)
-    flipped = dot_tn(taps_in, (col_m == taps - row_j).astype(BF16))
-    straight = dot_tn(taps_in, (col_m == row_j).astype(BF16))
+    flipped = jnp.dot(
+        taps_in, (col_m == taps - row_j).astype(BF16), preferred_element_type=F32
+    )
+    straight = jnp.dot(taps_in, (col_m == row_j).astype(BF16), preferred_element_type=F32)
     spread = (iota((groups, tiles * LANES), 1) // width == iota((groups, tiles * LANES), 0))
     wide = jnp.dot(sf_ref[0], spread.astype(BF16), preferred_element_type=F32)
     for k in range(tiles):
@@ -139,7 +147,7 @@
         ef[:, :, rows : rows + RIM] = jnp.zeros((tiles, features, RIM, LANES), F32)
 
     def zero_copy():
-        return pltpu.make_async_copy(zb, out_ref.at[0], z_sem.at[0])
+        return pltpu.make_async_copy(zb, out_ref, z_sem.at[0])
 
     @pl.when(jnp.logical_not(gets_out))
     def _():
@@ -152,11 +160,14 @@
     def _():
         x_copy().wait_recv()
 
+    load_x().wait()
+    load_gy().wait()
+
     def lane_slice(k):
         return pl.ds(pl.multiple_of(k * LANES, LANES), LANES)
 
     def feature_tile(k, carry):
-        xf[k, RIM : RIM + rows] = x_ref[0, :, lane_slice(k)].astype(F32)
+        xf[k, RIM : RIM + rows] = xv[:, lane_slice(k)].astype(F32)
         xf[k, 0:RIM] = xrim[:, lane_slice(k)].astype(F32)[16 - RIM :]
         for start in range(0, rows, CHUNK):
             sums = [jnp.zeros((CHUNK, LANES), F32) for _ in range(features)]
@@ -172,7 +183,7 @@
                 key.astype(F32) * val.astype(F32)
             ).astype(BF16)
             gext[k, here] = (
-                gy_ref[0, here, lane_slice(k)].astype(F32) * q.astype(F32)
+                gyv[here, lane_slice(k)].astype(F32) * q.astype(F32)
             ).astype(BF16)
 
         @pl.when(has_next)
@@ -196,60 +207,63 @@
             [ref[k, b * taps : b * taps + span] for b in range(nb)], axis=1
         )
 
+    def medium_ready(k):
+        @pl.when(has_prev)
+        def _():
+            kv_copy(k).wait_recv()
+
+        @pl.when(has_next)
+        def _():
+            gate_copy(k).wait_recv()
+
+    def medium_sent(k):
+        @pl.when(has_prev)
+        def _():
+            rim_copy(k).start()
+
     def medium_tile(k):
-        @pl.when(has_prev)
-        def _():
-            kv_copy(k).wait_recv()
-
-        @pl.when(has_next)
-        def _():
-            gate_copy(k).wait_recv()
-
         kv_win = windows(kvp, k)
         gate_win = windows(gext, k)
-        mixed = jnp.zeros((taps, nb * LANES), F32)
-        back = jnp.zeros((taps, nb * LANES), F32)
-        for u in range(gpt):
-            cols = slice(u * span, (u + 1) * span)
-            mixed = mixed + jnp.dot(
-                tm[k, :, cols], kv_win * masks[u], preferred_element_type=F32
-            )
-            back = back + jnp.dot(
-                tk[k, :, cols], gate_win * masks[u], preferred_element_type=F32
-            )
+        kv_all = jnp.concatenate([kv_win * m for m in masks], axis=0)
+        mixed = jnp.dot(tm[k], kv_all, preferred_element_type=F32)
+        gate_all = jnp.concatenate([gate_win * m for m in masks], axis=0)
+        back = jnp.dot(tk[k], gate_all, preferred_element_type=F32)
         for b in range(nb):
             here = slice(b * taps, (b + 1) * taps)
             mix_b = mixed[:, b * LANES : (b + 1) * LANES]
             back_b = back[:, b * LANES : (b + 1) * LANES]
             ef[k, 0, here] = (
-                gy_ref[0, here, lane_slice(k)].astype(F32) * mix_b
+                gyv[here, lane_slice(k)].astype(F32) * mix_b
             ).astype(BF16).astype(F32)
             ef[k, 1, here] = (back_b * valb[k, here].astype(F32)).astype(BF16).astype(F32)
             ef[k, 2, here] = (back_b * keyb[k, here].astype(F32)).astype(BF16).astype(F32)
 
-        @pl.when(has_prev)
-        def _():
-            rim_copy(k).start()
-
         kv_own = jnp.concatenate(
             [kvp[k, taps + b * taps : span + b * taps] for b in range(nb)], axis=1
         )
         kv_rev = jnp.dot(reverse, kv_own, preferred_element_type=F32).astype(BF16)
         lines = []
+        crosses = dot_nt(jnp.concatenate([kv_rev * m for m in masks], axis=0), gate_win)
         for u in range(gpt):
-            cross = dot_nt(kv_rev * masks[u], gate_win)
+            cross = crosses[u * taps : (u + 1) * taps]
             turned = pltpu.roll(cross, 0, 1, stride=1, stride_axis=0)
             lines.append(jnp.sum(turned, axis=0, keepdims=True))
         diag = pltpu.roll(jnp.concatenate(lines, axis=0), span - taps + 1, 1)
-        grads[pl.ds(pl.multiple_of(k * gpt, gpt), gpt), 0:taps] = diag[:, 0:taps]
+        grads_m[pl.ds(pl.multiple_of(k * gpt, gpt), gpt), :] = diag[:, 0:taps]
 
     gather = (iota((gpt, LANES), 1) // width == iota((gpt, LANES), 0)).astype(F32)
 
+    def short_ready(k):
+        @pl.when(has_next)
+        def _():
+            rim_copy(k).wait_recv()
+
+    def short_sent(k):
+        @pl.when(sends_out)
+        def _():
+            out_copy(k).start()
+
     def short_tile(k):
-        @pl.when(has_next)
-        def _():
-            rim_copy(k).wait_recv()
-
         sums = [jnp.zeros((8, LANES), F32) for _ in range(features * lags)]
         for start in range(0, rows, CHUNK):
             x_here = xf[k, RIM + start : RIM + start + CHUNK]
@@ -264,34 +278,37 @@
                     )
             ot[k, start : start + CHUNK] = total.astype(BF16)
 
-        @pl.when(sends_out)
-        def _():
-            out_copy(k).start()
-
         flat = [jnp.sum(v, axis=0, keepdims=True) for v in sums]
         flat.append(jnp.zeros((LANES - features * lags, LANES), F32))
         flat = jnp.concatenate(flat, axis=0)
-        grads[pl.ds(pl.multiple_of(k * gpt, gpt), gpt), taps : taps + LANES] = dot_nt(
+        grads_s[pl.ds(pl.multiple_of(k * gpt, gpt), gpt), :] = dot_nt(
             gather, flat, precision=lax.Precision.HIGHEST
         )
 
     lag = 2
+    for k in range(lag):
+        medium_ready(k)
+        medium_tile(k)
+        medium_sent(k)
 
     def step(k, carry):
-        @pl.when(k < tiles)
-        def _():
-            medium_tile(k)
-
-        @pl.when(k >= lag)
-        def _():
-            short_tile(k - lag)
-
+        medium_ready(k)
+        short_ready(k - lag)
+        short_tile(k - lag)
+        medium_tile(k)
+        medium_sent(k)
+        short_sent(k - lag)
         return carry
 
-    lax.fori_loop(0, tiles + lag, step, 0)
+    lax.fori_loop(lag, tiles, step, 0)
+    for k in range(tiles - lag, tiles):
+        short_ready(k)
+        short_tile(k)
+        short_sent(k)
 
     for p in range(n_ctx):
-        snd[p] = grads[p * gpd : (p + 1) * gpd]
+        snd[p, :, 0:taps] = grads_m[p * gpd : (p + 1) * gpd]
+        snd[p, :, taps : taps + LANES] = grads_s[p * gpd : (p + 1) * gpd]
 
     def grad_copy(d):
         to = lax.rem(c + d, n_ctx)
@@ -303,10 +320,10 @@
     for d in range(1, n_ctx):
         grad_copy(d).wait_recv()
         total = total + rcv[d - 1]
+    gm_ref[0] = total[:, 0:taps]
     tr[...] = jnp.zeros_like(tr)
-    tr[0:gpd] = total
-    gm_ref[0] = tr[:, 0:taps].T[:, 0:gpd]
-    gs_ref[0] = tr[:, taps : taps + LANES].T[0 : features * lags, 0:gpd]
+    tr[0:gpd] = total[:, taps : taps + LANES]
+    gs_ref[:, 0] = tr[...].T[0 : features * lags, 0:gpd]
 
     for d in range(1, n_ctx):
         grad_copy(d).wait_send()
@@ -340,6 +357,21 @@
     @pl.when(jnp.logical_not(gets_out))
     def _():
         zero_copy().wait()
+
+
+def place(tiles, tiled_ref, gs_in, gm_in, out_ref, gs_ref, gm_ref, sem):
+    copies = [
+        pltpu.make_async_copy(
+            tiled_ref.at[k], out_ref.at[0, :, pl.ds(k * LANES, LANES)], sem.at[k]
+        )
+        for k in range(tiles)
+    ]
+    copies.append(pltpu.make_async_copy(gs_in, gs_ref, sem.at[tiles]))
+    copies.append(pltpu.make_async_copy(gm_in, gm_ref, sem.at[tiles + 1]))
+    for copy in copies:
+        copy.start()
+    for copy in copies:
+        copy.wait()
 
 
 def per_device(n_ctx, n_sec, inputs, upstream, short_filter, medium_filter):
@@ -354,16 +386,19 @@
     vmem = pl.BlockSpec(memory_space=pltpu.VMEM)
     dma = pltpu.SemaphoreType.DMA
     span = 2 * taps
-    return pl.pallas_call(
+    hbm = pl.BlockSpec(memory_space=pltpu.HBM)
+    incoming, short_part, medium_part = pl.pallas_call(
         partial(kernel, dims),
         out_shape=(
-            jax.ShapeDtypeStruct(inputs.shape, BF16),
-            jax.ShapeDtypeStruct((1, 3 * lags, gpd), F32),
-            jax.ShapeDtypeStruct((1, taps, gpd), F32),
+            jax.ShapeDtypeStruct((tiles, rows, LANES), BF16),
+            jax.ShapeDtypeStruct((3 * lags, 1, gpd), F32),
+            jax.ShapeDtypeStruct((1, gpd, taps), F32),
         ),
-        in_specs=[vmem] * 4,
+        in_specs=[hbm, hbm, vmem, vmem],
         out_specs=(pl.BlockSpec(memory_space=pl.ANY), vmem, vmem),
         scratch_shapes=[
+            pltpu.VMEM((rows, chans), BF16),
+            pltpu.VMEM((rows, chans), BF16),
             pltpu.VMEM((tiles, gpt, span), F32),
             pltpu.VMEM((tiles, gpt, span), F32),
             pltpu.VMEM((tiles, 24, LANES), F32),
@@ -377,11 +412,12 @@
             pltpu.VMEM((tiles, rows, LANES), BF16),
             pltpu.VMEM((tiles, 3, rows + RIM, LANES), F32),
             pltpu.VMEM((tiles, rows, LANES), BF16),
-            pltpu.VMEM((rows, chans), BF16),
-            pltpu.VMEM((groups, taps + LANES), F32),
+            pltpu.VMEM((tiles, rows, LANES), BF16),
+            pltpu.VMEM((groups, taps), F32),
+            pltpu.VMEM((groups, LANES), F32),
             pltpu.VMEM((n_ctx, gpd, taps + LANES), F32),
             pltpu.VMEM((max(n_ctx - 1, 1), gpd, taps + LANES), F32),
-            pltpu.VMEM((LANES, taps + LANES), F32),
+            pltpu.VMEM((LANES, LANES), F32),
             dma((1,)), dma((1,)),
             dma((tiles,)), dma((tiles,)),
             dma((tiles,)), dma((tiles,)),
@@ -389,11 +425,30 @@
             dma((tiles,)), dma((tiles,)),
             dma((max(n_ctx - 1, 1),)), dma((max(n_ctx - 1, 1),)),
             dma((1,)),
+            dma((2,)),
         ],
         compiler_params=pltpu.CompilerParams(
             collective_id=0, has_side_effects=True, vmem_limit_bytes=40 * 1024 * 1024
         ),
-    )(inputs, upstream, short_filter, medium_filter)
+    )(
+        pltpu.with_memory_space_constraint(inputs, pltpu.HBM),
+        pltpu.with_memory_space_constraint(upstream, pltpu.HBM),
+        pltpu.with_memory_space_constraint(short_filter, pltpu.HBM),
+        pltpu.with_memory_space_constraint(medium_filter.transpose(0, 2, 1), pltpu.HBM),
+    )
+    incoming, short_part, medium_part = pl.pallas_call(
+        partial(place, tiles),
+        out_shape=(
+            jax.ShapeDtypeStruct(inputs.shape, BF16),
+            jax.ShapeDtypeStruct(short_part.shape, F32),
+            jax.ShapeDtypeStruct(medium_part.shape, F32),
+        ),
+        in_specs=[pl.BlockSpec(memory_space=pl.ANY)] * 3,
+        out_specs=(hbm,) * 3,
+        scratch_shapes=[dma((tiles + 2,))],
+        compiler_params=pltpu.CompilerParams(vmem_limit_bytes=16 * 1024 * 1024),
+    )(incoming, short_part, medium_part)
+    return incoming, short_part.transpose(1, 0, 2), medium_part.transpose(0, 2, 1)
 
 
 def solution(mesh):

time: 33.1 us -> 29.1 us (0.88)
  local copies, waits for them, and re-layouts: 5 us -> 0 us
  Pallas kernels: 27.2 us -> 28.2 us
    unnamed x8 -> x0, local copies, waits for them, and re-layouts: 3.71 us -> none
    pallas_call x2 -> x0, local copies, waits for them, and re-layouts: 1.29 us -> none  [per_device(): pl.pallas_call(partial(kernel, dims), out_shape=(jax.ShapeDtypeStruct(inp...]
    pallas_call x1 -> x2, Pallas kernels: 27.2 us -> 28.2 us  [the longest x1 27.3 us: per_device(): pl.pallas_call(partial(kernel, dims), out_shape=(jax.ShapeDtypeStruct((ti...]
where the time goes in v2:
time: 29.1 us; the launch traced here: 28.8 us
  Pallas kernels  28.2 us (97%)
  between operations  0.64 us (2%)
    pallas_call x1, Pallas kernels, per_device(): pl.pallas_call(partial(kernel, dims), out_shape=(jax.ShapeDtypeStruct((ti...  27.3 us
    pallas_call x1, Pallas kernels, per_device(): pl.pallas_call(partial(place, tiles), out_shape=(jax.ShapeDtypeStruct(inp...  0.87 us

profile of v2, /device:TPU:1, one launch (start us, length us, event | category | flops | bytes accessed | tf_op | source)
XLA Modules:
  0.0 28.8 jit_solution(15881702481891316037)
XLA Ops:
  0.6 27.3 %shard_map.67 = (bf16[8,256,128]{2,1,0:T(8,128)(2,1)S(1)}, f32[21,1,32]{2,1,0:T(1,128)S(1)}, f32[1,32,128]{2,1,0:T(8,128)S(1)}) custom-call(bf16[1,256,1024]{2,1,0:T(8,128)(2,1)} %x_ref.1, bf16[1,256,1024]{2,1,0:T(8,128)(2,1)} %gy_ref.1, bf16[1,21,64]{2,1,0:T(8,128)(2,1)} %sf_ref.1, bf16[1,64,128]{2,1,0:T(8,128)(2,1)} %bitcast.3), custom_call_target="tpu_custom_call" | custom-call | tf_op jit(solution)/shard_map/pallas_call | solution.py:390
  28.0 0.9 %shard_map.68 = (bf16[1,256,1024]{2,1,0:T(8,128)(2,1)}, f32[21,1,32]{2,1,0:T(1,128)}, f32[1,32,128]{2,1,0:T(8,128)}) custom-call(bf16[8,256,128]{2,1,0:T(8,128)(2,1)S(1)} %get-tuple-element.9.tiled_ref, f32[21,1,32]{2,1,0:T(1,128)S(1)} %get-tuple-element.10.gs_in, f32[1,32,128]{2,1,0:T(8,128)S(1)} %get-tuple-element.11.gm_in), custom_call_target="tpu_custom_call" | custom-call | tf_op jit(solution)/shard_map/pallas_call | solution.py:439

commit v3 on v2

--- a/solution.py
+++ b/solution.py
@@ -166,7 +166,7 @@
     def lane_slice(k):
         return pl.ds(pl.multiple_of(k * LANES, LANES), LANES)
 
-    def feature_tile(k, carry):
+    def feature_tile(k):
         xf[k, RIM : RIM + rows] = xv[:, lane_slice(k)].astype(F32)
         xf[k, 0:RIM] = xrim[:, lane_slice(k)].astype(F32)[16 - RIM :]
         for start in range(0, rows, CHUNK):
@@ -186,6 +186,7 @@
                 gyv[here, lane_slice(k)].astype(F32) * q.astype(F32)
             ).astype(BF16)
 
+    def feature_sent(k):
         @pl.when(has_next)
         def _():
             kv_copy(k).start()
@@ -193,10 +194,6 @@
         @pl.when(has_prev)
         def _():
             gate_copy(k).start()
-
-        return carry
-
-    lax.fori_loop(0, tiles, feature_tile, 0)
 
     lane_group = lax.rem(iota((1, nb * LANES), 1), LANES) // width
     masks = [(lane_group == u).astype(BF16) for u in range(gpt)]
@@ -285,13 +282,26 @@
             gather, flat, precision=lax.Precision.HIGHEST
         )
 
-    lag = 2
-    for k in range(lag):
+    def feature_step(k, carry):
+        feature_tile(k)
+        feature_sent(k)
+        return carry
+
+    lax.fori_loop(0, tiles, feature_step, 0)
+
+    def medium_step(k, carry):
         medium_ready(k)
         medium_tile(k)
         medium_sent(k)
-
-    def step(k, carry):
+        return carry
+
+    def short_step(k, carry):
+        short_ready(k)
+        short_tile(k)
+        short_sent(k)
+        return carry
+
+    def both_step(k, carry):
         medium_ready(k)
         short_ready(k - lag)
         short_tile(k - lag)
@@ -300,11 +310,10 @@
         short_sent(k - lag)
         return carry
 
-    lax.fori_loop(lag, tiles, step, 0)
-    for k in range(tiles - lag, tiles):
-        short_ready(k)
-        short_tile(k)
-        short_sent(k)
+    lag = 4
+    lax.fori_loop(0, lag, medium_step, 0)
+    lax.fori_loop(lag, tiles, both_step, 0)
+    lax.fori_loop(tiles - lag, tiles, short_step, 0)
 
     for p in range(n_ctx):
         snd[p, :, 0:taps] = grads_m[p * gpd : (p + 1) * gpd]

time: 29.1 us -> 28.1 us (0.966)
  Pallas kernels: 28.2 us -> 27.2 us
    pallas_call x1, Pallas kernels: 27.3 us -> 26.3 us  [per_device(): pl.pallas_call(partial(kernel, dims), out_shape=(jax.ShapeDtypeStruct((ti...]
where the time goes in v3:
time: 28.1 us; the launch traced here: 27.9 us
  Pallas kernels  27.2 us (97%)
  between operations  0.64 us (2%)
    pallas_call x1, Pallas kernels, per_device(): pl.pallas_call(partial(kernel, dims), out_shape=(jax.ShapeDtypeStruct((ti...  26.3 us
    pallas_call x1, Pallas kernels, per_device(): pl.pallas_call(partial(place, tiles), out_shape=(jax.ShapeDtypeStruct(inp...  0.87 us

profile of v3, /device:TPU:1, one launch (start us, length us, event | category | flops | bytes accessed | tf_op | source)
XLA Modules:
  0.0 27.9 jit_solution(13117802061812935876)
XLA Ops:
  0.6 26.3 %shard_map.67 = (bf16[8,256,128]{2,1,0:T(8,128)(2,1)S(1)}, f32[21,1,32]{2,1,0:T(1,128)S(1)}, f32[1,32,128]{2,1,0:T(8,128)S(1)}) custom-call(bf16[1,256,1024]{2,1,0:T(8,128)(2,1)} %x_ref.1, bf16[1,256,1024]{2,1,0:T(8,128)(2,1)} %gy_ref.1, bf16[1,21,64]{2,1,0:T(8,128)(2,1)} %sf_ref.1, bf16[1,64,128]{2,1,0:T(8,128)(2,1)} %bitcast.3), custom_call_target="tpu_custom_call" | custom-call | tf_op jit(solution)/shard_map/pallas_call | solution.py:399
  27.0 0.9 %shard_map.68 = (bf16[1,256,1024]{2,1,0:T(8,128)(2,1)}, f32[21,1,32]{2,1,0:T(1,128)}, f32[1,32,128]{2,1,0:T(8,128)}) custom-call(bf16[8,256,128]{2,1,0:T(8,128)(2,1)S(1)} %get-tuple-element.9.tiled_ref, f32[21,1,32]{2,1,0:T(1,128)S(1)} %get-tuple-element.10.gs_in, f32[1,32,128]{2,1,0:T(8,128)S(1)} %get-tuple-element.11.gm_in), custom_call_target="tpu_custom_call" | custom-call | tf_op jit(solution)/shard_map/pallas_call | solution.py:448
